TPU v7x, 512 devices: a whole 4x4x16 slice. The times are simulated.
512 devices in a mesh: ctx: 64 (over y, z), ch: 8 (over x, core).
Axes of the slice: x: 4, y: 4, z: 16, core: 2. Of those that a mesh axis runs over, the one named last changes fastest.
Arguments:
- query_rows: bfloat16 [8192, 8192], P('ctx', 'ch'), may hold values from -6 to 6
- key_rows: bfloat16 [8192, 8192], P('ctx', 'ch'), may hold values from -6 to 6
- value_rows: bfloat16 [8192, 8192], P('ctx', 'ch'), may hold values from -6 to 6
- short_filter: float32 [3, 3, 8192], P(None, None, 'ch'), may hold values from -3.5 to 3.5
- decay_rate: float32 [8192, 16], P('ch'), may hold values from 2e-05 to 0.1
- residues: float32 [8192, 16], P('ch'), may hold values from -1.5 to 1.5
- out_weight: bfloat16 [8192, 4096], P('ctx', 'ch'), may hold values from -0.1875 to 0.1875
- record_starts: int32 [4], replicated, may hold values from 0 to 8191, as said below
Outputs:
- block_out: bfloat16 [8192, 4096], P('ctx', 'ch')
Inputs may be any that keep to these rules, and one draw needn't show every extreme that they name: record_starts[0] is 0 and the last entry is 8191; the entries are distinct and increasing, and all but the first lie in the second half of the 8192 tokens.
All inputs are finite; a program needn't handle non-finite values.
Results may differ from a plain program's by a relative error of at most 0.017.
Values may be sent and summed in bfloat16 or wider, within the bound.
A program may use at most 64 MiB of HBM per device.

v0:
```python
import jax
import jax.numpy as jnp
from jax import lax
from jax.sharding import PartitionSpec as P

MODES = 16
KS = 3


def shifted(block, axis, distance):
    devices = range(lax.axis_size(axis))
    route = [(i - distance, i) for i in devices if i - distance in devices]
    return lax.ppermute(block, axis, route)


def carried_in(x, axis, combine, identity):
    devices, mine = (lax.axis_size(axis), lax.axis_index(axis))
    everything = jax.tree.map(lambda part: lax.all_gather(part, axis), x)
    start = jax.tree.map(
        lambda part, zero: jnp.broadcast_to(jnp.asarray(zero, part.dtype), part.shape), x, identity
    )

    def hop(k, before):
        reached = k < mine
        new = combine(before, jax.tree.map(lambda part: part[k], everything))
        return jax.tree.map(lambda a, b: jnp.where(reached, a, b), new, before)

    return lax.fori_loop(0, devices, hop, start)


def ages_of(positions, record_starts):
    earlier = record_starts[None, :] <= positions[:, None]
    segment = jnp.max(jnp.where(earlier, record_starts[None, :], 0), axis=1)
    return positions - segment


def masked_conv(extended, weights, ages, count):
    taps = weights.shape[0]
    total = jnp.zeros((count, extended.shape[1]), jnp.float32)
    for tap_index in range(taps):
        keeper = (ages >= tap_index).astype(jnp.float32)[:, None]
        window = extended[taps - 1 - tap_index : taps - 1 - tap_index + count]
        total = total + weights[tap_index][None, :] * window * keeper
    return total


def combine_pairs(earlier, later_pair):
    return (earlier[0] * later_pair[0], later_pair[0] * earlier[1] + later_pair[1])


def local(
    query_rows, key_rows, value_rows, short_filter, decay_rate, residues, out_weight, record_starts
):
    row_count, channels = query_rows.shape
    anchor = lax.axis_index("ctx") * row_count
    positions = anchor + jnp.arange(row_count, dtype=jnp.int32)
    ages = ages_of(positions, record_starts)
    reach_short = KS - 1
    tails = shifted(
        (
            query_rows[row_count - reach_short :],
            key_rows[row_count - reach_short :],
            value_rows[row_count - reach_short :],
        ),
        "ctx",
        1,
    )
    query_conv = masked_conv(
        jnp.concatenate([tails[0], query_rows], axis=0).astype(jnp.float32),
        short_filter[0],
        ages,
        row_count,
    )
    key_conv = masked_conv(
        jnp.concatenate([tails[1], key_rows], axis=0).astype(jnp.float32),
        short_filter[1],
        ages,
        row_count,
    )
    value_conv = masked_conv(
        jnp.concatenate([tails[2], value_rows], axis=0).astype(jnp.float32),
        short_filter[2],
        ages,
        row_count,
    )
    mixed = (key_conv * value_conv).astype(jnp.bfloat16).astype(jnp.float32)
    gain = jnp.sqrt(1.0 - jnp.exp(-2.0 * decay_rate))
    block_rows = 8
    block_count = row_count // block_rows
    inner_index = jnp.arange(block_rows, dtype=jnp.float32)
    inner_ints = jnp.arange(block_rows, dtype=jnp.int32)
    rising = jnp.exp(-decay_rate[None, :, :] * inner_index[:, None, None])
    taps_inner = jnp.sum(rising * (residues * gain)[None, :, :], axis=2)
    local_index = jnp.arange(row_count, dtype=jnp.int32)
    inner_ages = jnp.minimum(ages, local_index % block_rows)
    padded_mixed = jnp.concatenate(
        [jnp.zeros((block_rows - 1, channels), jnp.float32), mixed], axis=0
    )
    within = masked_conv(padded_mixed, taps_inner, inner_ages, row_count)
    entry_powers = jnp.exp(-decay_rate[None, :, :] * (inner_index[:, None, None] + 1.0))
    final_powers = (
        jnp.exp(-decay_rate[None, :, :] * (block_rows - 1.0 - inner_index[:, None, None]))
        * gain[None, :, :]
    )
    block_decay = jnp.exp(-decay_rate * block_rows)
    mixed_blocks = mixed.reshape(block_count, block_rows, channels)
    age_blocks = ages.reshape(block_count, block_rows)
    last_ages = age_blocks[:, block_rows - 1]
    weighted = (last_ages[:, None] >= block_rows - 1 - inner_ints[None, :]).astype(jnp.float32)
    endings = jnp.einsum("rcm,brc->bcm", final_powers, mixed_blocks * weighted[:, :, None])
    unbroken = (last_ages >= block_rows).astype(jnp.float32)

    def advance(state, inputs):
        ending, kept = inputs
        return (block_decay * kept * state + ending, state)

    local_state, entering_states = lax.scan(
        advance, jnp.zeros((channels, MODES), jnp.float32), (endings, unbroken)
    )
    entering = (age_blocks > inner_ints[None, :]).astype(jnp.float32)
    between = (
        jnp.einsum("rcm,bcm->brc", entry_powers, residues[None, :, :] * entering_states)
        * entering[:, :, None]
    )
    device_decay = jnp.exp(-decay_rate * row_count) * (ages[row_count - 1] >= row_count).astype(
        jnp.float32
    )
    identity_pair = (jnp.ones_like(device_decay), jnp.zeros_like(local_state))
    carried = carried_in((device_decay, local_state), "ctx", combine_pairs, identity_pair)[1]
    block_index = jnp.arange(block_count, dtype=jnp.float32)
    block_starts = jnp.exp(-decay_rate[None, :, :] * (block_index[:, None, None] * block_rows))
    coefficient = block_starts * (residues * carried)[None, :, :]
    correction = jnp.einsum("rcm,bcm->brc", entry_powers, coefficient).reshape(row_count, channels)
    untouched = (ages > local_index).astype(jnp.float32)[:, None]
    filtered = within + between.reshape(row_count, channels) + correction * untouched
    gated = (query_conv * filtered).astype(jnp.bfloat16)
    all_channels = lax.all_gather(gated, "ch", axis=1, tiled=True)
    result = jnp.dot(
        all_channels,
        lax.all_gather(out_weight, "ctx", axis=0, tiled=True),
        preferred_element_type=jnp.float32,
    )
    return result.astype(jnp.bfloat16)


def solution(mesh):
    return jax.shard_map(
        local,
        mesh=mesh,
        in_specs=(
            P("ctx", "ch"),
            P("ctx", "ch"),
            P("ctx", "ch"),
            P(None, None, "ch"),
            P("ch", None),
            P("ch", None),
            P("ctx", "ch"),
            P(),
        ),
        out_specs=P("ctx", "ch"),
        check_vma=False,
    )
```

profile of v0, /device:TPU:32, one launch (start us, length us, event | category | flops | bytes accessed | tf_op | source)
XLA Modules:
  0.0 616.6 jit_solution(5873278730106274515)
XLA Ops:
  7.3 3.8 collective-permute-start.1
  11.8 3.8 collective-permute-start.2
  17.6 1.6 fusion.59
  23.6 2.8 copy.59
  26.3 5.7 fusion.16
  32.1 5.2 copy.61
  37.3 32.3 %while.27 = (s32[]{:T(128)}, f32[1024,16]{0,1:T(8,128)S(1)}, f32[16,1024,16]{1,2,0:T(8,128)}, f32[16]{0:T(128)S(1)}, f32[1024,16]{0,1:T(8,128)S(1)}, /*index=5*/f32[16,1024,16]{1,2,0:T(8,128)S(1)}, s32[]{:T(128)}, s32[]{:T(128)}) while((s32[]{:T(128)}, f32[1024,16]{0,1:T(8,128)S(1)}, f32[16,1024,16]{1,2,0:T(8,128)}, ...), condition=%wide.region_3.4_spmd.clone, body=%wide.region_2.3_spmd.clone.sunk | while | flops 81923 | bytes 393844 | solution.py:117
  70.3 5.0 collective-permute-start
  76.8 2.1 slice_reduce_fusion.7
  79.1 4.9 copy.62
  84.0 6.5 %multiply_bitcast_fusion = f32[16,8,1024]{0,1,2:T(8,128)} fusion(bf16[16,1024,16]{2,0,1:T(8,128)(2,1)} %copy.62, f32[16,8]{0,1:T(8,128)S(1)} %copy.63, f32[8]{0:T(128)S(1)} %iota_add_fusion, f32[1024,16]{1,0:T(8,128)S(1)} %copy.57), kind=kOutput, calls=%fused_computation.16 | convolution fusion | flops 4456448 | bytes 1114656 | tf_op jit(solution)/shard_map/rcm,bcm->brc/dot_general | solution.py:122
  90.5 3.0 copy.64
  93.6 74.4 %all-gather.11.cloned.1.call-done = f32[65536,16]{0,1:T(8,128)} async-done(((f32[1024,16]{0,1:T(8,128)}), f32[65536,16]{0,1:T(8,128)}) %all-gather.11.cloned.1.call-update) | async-done | bytes 4194320 | tf_op jit(solution)/shard_map/all_gather | solution.py:18
  168.0 6.5 %copy.72 = f32[2,8,64,1024]{3,2,1,0:T(8,128)} copy(f32[2,8,64,1024]{3,1,2,0:T(8,128)} %bitcast.68) | data formatting | bytes 8388608
  174.5 137.7 %all-gather.13.cloned.1.call-done = f32[65536,16]{0,1:T(8,128)} async-done(((f32[1024,16]{0,1:T(8,128)}), f32[65536,16]{0,1:T(8,128)}) %all-gather.13.cloned.1.call-update) | async-done | bytes 4194320 | tf_op jit(solution)/shard_map/all_gather | solution.py:18
  312.3 6.6 %copy.73 = f32[2,8,64,1024]{3,2,1,0:T(8,128)} copy(f32[2,8,64,1024]{3,1,2,0:T(8,128)} %bitcast.69) | data formatting | bytes 8388608
  318.9 88.1 %while.28 = (s32[]{:T(128)}, f32[1024,16]{0,1:T(8,128)S(1)}, s32[]{:T(128)}, f32[64,1024,16]{1,0,2:T(8,128)}, f32[64,1024,16]{1,0,2:T(8,128)}, /*index=5*/s32[]{:T(128)}, s32[]{:T(128)}) while((s32[]{:T(128)}, f32[1024,16]{0,1:T(8,128)S(1)}, s32[]{:T(128)}, f32[64,1024,16]{1,0,2:T(8,128)}, f32[64,1024,16]{1,0,2:T(8,128)}, ...), condition=%wide.region_5.6_spmd.clone, body=%wide.region_4.5_spmd.clone.sunk | while | flops 65540 | bytes 524389 | solution.py:28
  320.2 1.3 constant_dynamic-slice_fusion.3
  321.6 1.3 constant_dynamic-slice_fusion.3
  323.0 1.3 constant_dynamic-slice_fusion.3
  324.4 1.3 constant_dynamic-slice_fusion.3
  325.7 1.3 constant_dynamic-slice_fusion.3
  327.1 1.3 constant_dynamic-slice_fusion.3
  328.5 1.3 constant_dynamic-slice_fusion.3
  329.9 1.3 constant_dynamic-slice_fusion.3
  331.2 1.3 constant_dynamic-slice_fusion.3
  407.2 3.9 fusion.21
  411.0 3.0 copy.69
  414.0 1.7 fusion.47
  416.3 27.3 %all-gather.7.cloned.1.call-done = bf16[128,8192]{1,0:T(8,128)(2,1)} async-done(((bf16[128,1024]{1,0:T(8,128)(2,1)}), bf16[128,8192]{1,0:T(8,128)(2,1)}) %all-gather.7.cloned.1.call-update) | async-done | bytes 2097168 | tf_op jit(solution)/shard_map/all_gather | solution.py:137
  443.7 160.5 %all-gather.9.cloned.1.call-done = bf16[8192,512]{1,0:T(8,128)(2,1)} async-done(((bf16[128,512]{1,0:T(8,128)(2,1)}), bf16[8192,512]{1,0:T(8,128)(2,1)}) %all-gather.9.cloned.1.call-update) | async-done | bytes 8388624 | tf_op jit(solution)/shard_map/all_gather | solution.py:140
  604.1 5.9 convolution_convert_fusion
  (219 shorter events, 116.6 us)
Async XLA Ops:
  6.5 161.5 %all-gather.11.cloned.1.call-start = ((), (), s32[]{:S(2)}) async-start(), calls=%async_computation.2 | async-start | bytes 4259840 | tf_op jit(solution)/shard_map/all_gather | solution.py:18
  7.3 13.7 %collective-permute-start.1 = (bf16[2,1024]{1,0:T(2,128)(2,1)S(1)}, bf16[2,1024]{1,0:T(2,128)(2,1)S(1)}, u32[]{:S(2)}, u32[]{:S(2)}) collective-permute-start(bf16[2,1024]{1,0:T(2,128)(2,1)S(1)} %slice.146), channel_id=1, source_target_pairs={{0,8},{8,16},{16,24},{24,32},{32,40},{40,48},{48,56},{56,64},{64,7... | collective-permute-start | bytes 12296 | tf_op jit(solution)/shard_map/ppermute | solution.py:13
  11.8 10.2 %collective-permute-start.2 = (bf16[2,1024]{1,0:T(2,128)(2,1)S(1)}, bf16[2,1024]{1,0:T(2,128)(2,1)S(1)}, u32[]{:S(2)}, u32[]{:S(2)}) collective-permute-start(bf16[2,1024]{1,0:T(2,128)(2,1)S(1)} %slice.153), channel_id=1, source_target_pairs={{0,8},{8,16},{16,24},{24,32},{32,40},{40,48},{48,56},{56,64},{64,7... | collective-permute-start | bytes 12296 | tf_op jit(solution)/shard_map/ppermute | solution.py:13
  19.2 293.1 %all-gather.13.cloned.1.call-start = ((), (), s32[]{:S(2)}) async-start(), calls=%async_computation.3 | async-start | bytes 4259840 | tf_op jit(solution)/shard_map/all_gather | solution.py:18
  32.1 38.2 %copy-start.3 = (bf16[128,1024]{1,0:T(8,128)(2,1)S(1)}, bf16[128,1024]{1,0:T(8,128)(2,1)}, u32[]{:S(2)}) copy-start(bf16[128,1024]{1,0:T(8,128)(2,1)} %param.12) | copy-start | bytes 786436
  37.3 41.7 %copy-start.2 = (f32[1024,16]{0,1:T(8,128)S(1)}, f32[1024,16]{0,1:T(8,128)}, u32[]{:S(2)}) copy-start(f32[1024,16]{0,1:T(8,128)} %param.17) | copy-start | bytes 196612
  69.6 0.6 copy-start
  69.6 9.4 %copy-start.1 = (f32[16,1024,16]{1,2,0:T(8,128)S(1)}, f32[16,1024,16]{1,2,0:T(8,128)}, u32[]{:S(2)}) copy-start(f32[16,1024,16]{1,2,0:T(8,128)} %get-tuple-element.132) | copy-start | bytes 3145732
  70.2 373.5 %all-gather.7.cloned.1.call-start = ((), (), s32[]{:S(2)}) async-start(), calls=%async_computation | async-start | bytes 2359296 | tf_op jit(solution)/shard_map/all_gather | solution.py:137
  70.3 23.2 %collective-permute-start = (bf16[2,1024]{1,0:T(2,128)(2,1)S(1)}, bf16[2,1024]{1,0:T(2,128)(2,1)S(1)}, u32[]{:S(2)}, u32[]{:S(2)}) collective-permute-start(bf16[2,1024]{1,0:T(2,128)(2,1)S(1)} %slice.138), channel_id=1, source_target_pairs={{0,8},{8,16},{16,24},{24,32},{32,40},{40,48},{48,56},{56,64},{64,7... | collective-permute-start | bytes 12296 | tf_op jit(solution)/shard_map/ppermute | solution.py:13
  415.8 188.4 %all-gather.9.cloned.1.call-start = ((), (), s32[]{:S(2)}) async-start(), calls=%async_computation.1 | async-start | bytes 8519680 | tf_op jit(solution)/shard_map/all_gather | solution.py:140
Sparse Core Ops, SparseCore 0:
  19.3 148.6 all-gather.10
  171.0 141.2 all-gather.12
  415.9 27.7 all-gather.6
  446.5 157.6 all-gather.8
where the time goes:
time: 619 us; the launch traced here: 617 us
  waiting for transfers between devices  401 us (65%)
  local copies, waits for them, and re-layouts  133 us (21%)
  other arithmetic  32.3 us (5%)
  matrix products  22.1 us (4%)
  between operations  14.1 us (2%)
  starting transfers between devices  12.8 us (2%)
    all_gather x2, waiting for transfers between devices, carried_in(): everything = jax.tree.map(lambda part: lax.all_gather(part, axis), x)  212 us
    all_gather x1, waiting for transfers between devices, local(): lax.all_gather(out_weight, 'ctx', axis=0, tiled=True)  160 us
    dynamic_slice x64, local copies, waits for them, and re-layouts, hop(): new = combine(before, jax.tree.map(lambda part: part[k], everything))  83.4 us
    all_gather x1, waiting for transfers between devices, local(): all_channels = lax.all_gather(gated, 'ch', axis=1, tiled=True)  27.3 us
    unnamed x11, local copies, waits for them, and re-layouts  18.9 us
    ppermute x3, starting transfers between devices, shifted(): return lax.ppermute(block, axis, route)  12.7 us
  transfers between devices with their start and end apart: 7, of which 4 were waited for; matrix products, arithmetic and copies ran while one was open for 13% of the time, Pallas kernels for 0%

commit v1 on v0

--- a/solution.py
+++ b/solution.py
@@ -134,7 +134,12 @@
     untouched = (ages > local_index).astype(jnp.float32)[:, None]
     filtered = within + between.reshape(row_count, channels) + correction * untouched
     gated = (query_conv * filtered).astype(jnp.bfloat16)
-    all_channels = lax.all_gather(gated, "ch", axis=1, tiled=True)
+    ring = [gated]
+    for hop_ in range(7):
+        ring.append(lax.ppermute(ring[-1], "ch", [(dev, (dev + 1) % 8) for dev in range(8)]))
+    all_channels = jnp.roll(
+        jnp.concatenate(ring[::-1], axis=1), (lax.axis_index("ch") + 1) * ring[0].shape[1], axis=1
+    )
     result = jnp.dot(
         all_channels,
         lax.all_gather(out_weight, "ctx", axis=0, tiled=True),

time: 619 us -> 492 us (0.79)
  waiting for transfers between devices: 401 us -> 263 us
  local copies, waits for them, and re-layouts: 133 us -> 145 us
    all_gather x1, waiting for transfers between devices: 160 us -> 0.01 us  [local(): lax.all_gather(out_weight, 'ctx', axis=0, tiled=True)]
    ppermute x0 -> x7, waiting for transfers between devices: none -> 49 us  [local(): lax.ppermute(ring[-1], 'ch', [(dev, (dev + 1) % 8) for dev in range(8)])]
    all_gather x1 -> x0, waiting for transfers between devices: 27.3 us -> none  [local(): all_channels = lax.all_gather(gated, 'ch', axis=1, tiled=True)]
    unnamed x11 -> x26, local copies, waits for them, and re-layouts: 18.9 us -> 30.3 us
  transfers between devices with their start and end apart: 7 -> 13, of which waited for: 4 -> 9; matrix products, arithmetic and copies ran while one was open for 13% -> 39% of each run, Pallas kernels for 0% -> 0%
where the time goes in v1:
time: 492 us; the launch traced here: 489 us
  waiting for transfers between devices  263 us (53%)
  local copies, waits for them, and re-layouts  145 us (29%)
  other arithmetic  30.7 us (6%)
  matrix products  22.1 us (4%)
  between operations  14.1 us (3%)
  starting transfers between devices  12.8 us (3%)
    all_gather x2, waiting for transfers between devices, carried_in(): everything = jax.tree.map(lambda part: lax.all_gather(part, axis), x)  214 us
    dynamic_slice x64, local copies, waits for them, and re-layouts, hop(): new = combine(before, jax.tree.map(lambda part: part[k], everything))  83.8 us
    ppermute x7, waiting for transfers between devices, local(): lax.ppermute(ring[-1], 'ch', [(dev, (dev + 1) % 8) for dev in range(8)])  49 us
    unnamed x26, local copies, waits for them, and re-layouts  30.3 us
    ppermute x3, starting transfers between devices, shifted(): return lax.ppermute(block, axis, route)  12.7 us
    add x16, other arithmetic, advance(): return (block_decay * kept * state + ending, state)  10.4 us
    dynamic_update_slice x16, other arithmetic, local(): lax.scan(advance, jnp.zeros((channels, MODES), jnp.float32), (endings, un...  10 us
  transfers between devices with their start and end apart: 13, of which 9 were waited for; matrix products, arithmetic and copies ran while one was open for 39% of the time, Pallas kernels for 0%

profile of v1, /device:TPU:32, one launch (start us, length us, event | category | flops | bytes accessed | tf_op | source)
XLA Modules:
  0.0 489.3 jit_solution(255535532311788185)
XLA Ops:
  7.3 3.8 collective-permute-start.1
  11.8 3.8 collective-permute-start.2
  17.6 1.6 fusion.65
  23.6 2.8 copy.59
  26.3 5.7 %fusion.16 = f32[16,1024,16]{2,0,1:T(8,128)} fusion(f32[16,8,1024]{0,1,2:T(8,128)} %copy.59, f32[1024,16]{1,0:T(8,128)S(1)} %copy.60, f32[8]{0:T(128)S(1)} %iota_subtract_fusion, f32[16,8]{0,1:T(8,128)S(1)} %compare_convert_fusion, f32[1024,16]{1,0:T(8,128)S(1)} %copy.57), kind=kOutput, calls=%fused_computation.25 | convolution fusion | flops 4587520 | bytes 1704480 | tf_op jit(solution)/shard_map/rcm,brc->bcm/dot_general | solution.py:110
  32.1 5.2 %copy.61 = f32[16,1024,16]{1,2,0:T(8,128)S(1)} copy(f32[16,1024,16]{2,0,1:T(8,128)} %fusion.16) | data formatting | bytes 2097152
  37.3 30.5 %while.27 = (s32[]{:T(128)}, f32[1024,16]{0,1:T(8,128)S(1)}, f32[16,1024,16]{1,2,0:T(8,128)}, f32[16]{0:T(128)S(1)}, f32[1024,16]{0,1:T(8,128)S(1)}, /*index=5*/f32[16,1024,16]{1,2,0:T(8,128)S(1)}, s32[]{:T(128)}, s32[]{:T(128)}) while((s32[]{:T(128)}, f32[1024,16]{0,1:T(8,128)S(1)}, f32[16,1024,16]{1,2,0:T(8,128)}, ...), condition=%wide.region_3.4_spmd.clone, body=%wide.region_2.3_spmd.clone.sunk | while | flops 81923 | bytes 393844 | solution.py:117
  68.5 5.0 %collective-permute-start = (bf16[2,1024]{1,0:T(2,128)(2,1)S(1)}, bf16[2,1024]{1,0:T(2,128)(2,1)S(1)}, u32[]{:S(2)}, u32[]{:S(2)}) collective-permute-start(bf16[2,1024]{1,0:T(2,128)(2,1)S(1)} %slice.138), channel_id=1, source_target_pairs={{0,8},{8,16},{16,24},{24,32},{32,40},{40,48},{48,56},{56,64},{64,7... | collective-permute-start | bytes 12296 | tf_op jit(solution)/shard_map/ppermute | solution.py:13
  75.1 2.1 slice_reduce_fusion.7
  77.4 4.9 %copy.62 = bf16[16,1024,16]{2,0,1:T(8,128)(2,1)} copy(bf16[16,1024,16]{1,2,0:T(8,128)(2,1)S(1)} %broadcast_multiply_fusion) | data formatting | bytes 1048576 | tf_op jit(solution)/shard_map/mul | solution.py:122
  82.3 6.5 %multiply_bitcast_fusion = f32[16,8,1024]{0,1,2:T(8,128)} fusion(bf16[16,1024,16]{2,0,1:T(8,128)(2,1)} %copy.62, f32[16,8]{0,1:T(8,128)S(1)} %copy.63, f32[8]{0:T(128)S(1)} %iota_add_fusion, f32[1024,16]{1,0:T(8,128)S(1)} %copy.57), kind=kOutput, calls=%fused_computation.16 | convolution fusion | flops 4456448 | bytes 1114656 | tf_op jit(solution)/shard_map/rcm,bcm->brc/dot_general | solution.py:122
  88.8 3.0 copy.64
  91.9 76.0 %all-gather.8.cloned.1.call-done = f32[65536,16]{0,1:T(8,128)} async-done(((f32[1024,16]{0,1:T(8,128)}), f32[65536,16]{0,1:T(8,128)}) %all-gather.8.cloned.1.call-update) | async-done | bytes 4194320 | tf_op jit(solution)/shard_map/all_gather | solution.py:18
  167.9 6.6 %copy.72 = f32[2,8,64,1024]{3,2,1,0:T(8,128)} copy(f32[2,8,64,1024]{3,1,2,0:T(8,128)} %bitcast.67) | data formatting | bytes 8388608
  174.5 137.7 %all-gather.10.cloned.1.call-done = f32[65536,16]{0,1:T(8,128)} async-done(((f32[1024,16]{0,1:T(8,128)}), f32[65536,16]{0,1:T(8,128)}) %all-gather.10.cloned.1.call-update) | async-done | bytes 4194320 | tf_op jit(solution)/shard_map/all_gather | solution.py:18
  312.2 6.6 %copy.73 = f32[2,8,64,1024]{3,2,1,0:T(8,128)} copy(f32[2,8,64,1024]{3,1,2,0:T(8,128)} %bitcast.68) | data formatting | bytes 8388608
  318.8 88.4 %while.28 = (s32[]{:T(128)}, f32[1024,16]{0,1:T(8,128)S(1)}, s32[]{:T(128)}, f32[64,1024,16]{1,0,2:T(8,128)}, f32[64,1024,16]{1,0,2:T(8,128)}, /*index=5*/s32[]{:T(128)}, s32[]{:T(128)}) while((s32[]{:T(128)}, f32[1024,16]{0,1:T(8,128)S(1)}, s32[]{:T(128)}, f32[64,1024,16]{1,0,2:T(8,128)}, f32[64,1024,16]{1,0,2:T(8,128)}, ...), condition=%wide.region_5.6_spmd.clone, body=%wide.region_4.5_spmd.clone.sunk | while | flops 65540 | bytes 524389 | solution.py:28
  331.2 1.3 constant_dynamic-slice_fusion.3
  343.6 1.3 constant_dynamic-slice_fusion.3
  395.9 1.5 constant_dynamic-slice_fusion.3
  403.0 1.3 constant_dynamic-slice_fusion.3
  405.8 1.3 constant_dynamic-slice_fusion.3
  407.4 3.9 fusion.21
  411.3 3.3 copy.69
  415.7 7.0 %collective-permute-done.3 = bf16[128,1024]{1,0:T(8,128)(2,1)S(1)} collective-permute-done((bf16[128,1024]{1,0:T(8,128)(2,1)S(1)}, bf16[128,1024]{1,0:T(8,128)(2,1)S(1)}, u32[]{:S(2)}, u32[]{:S(2)}) %collective-permute-start.3) | collective-permute-done | bytes 262176 | tf_op jit(solution)/shard_map/ppermute | solution.py:139
  422.7 7.0 %collective-permute-done.4 = bf16[128,1024]{1,0:T(8,128)(2,1)S(1)} collective-permute-done((bf16[128,1024]{1,0:T(8,128)(2,1)S(1)}, bf16[128,1024]{1,0:T(8,128)(2,1)S(1)}, u32[]{:S(2)}, u32[]{:S(2)}) %collective-permute-start.4) | collective-permute-done | bytes 262176 | tf_op jit(solution)/shard_map/ppermute | solution.py:139
  429.7 7.0 %collective-permute-done.5 = bf16[128,1024]{1,0:T(8,128)(2,1)S(1)} collective-permute-done((bf16[128,1024]{1,0:T(8,128)(2,1)S(1)}, bf16[128,1024]{1,0:T(8,128)(2,1)S(1)}, u32[]{:S(2)}, u32[]{:S(2)}) %collective-permute-start.5) | collective-permute-done | bytes 262176 | tf_op jit(solution)/shard_map/ppermute | solution.py:139
  436.7 7.0 %collective-permute-done.6 = bf16[128,1024]{1,0:T(8,128)(2,1)S(1)} collective-permute-done((bf16[128,1024]{1,0:T(8,128)(2,1)S(1)}, bf16[128,1024]{1,0:T(8,128)(2,1)S(1)}, u32[]{:S(2)}, u32[]{:S(2)}) %collective-permute-start.6) | collective-permute-done | bytes 262176 | tf_op jit(solution)/shard_map/ppermute | solution.py:139
  443.7 7.0 %collective-permute-done.7 = bf16[128,1024]{1,0:T(8,128)(2,1)S(1)} collective-permute-done((bf16[128,1024]{1,0:T(8,128)(2,1)S(1)}, bf16[128,1024]{1,0:T(8,128)(2,1)S(1)}, u32[]{:S(2)}, u32[]{:S(2)}) %collective-permute-start.7) | collective-permute-done | bytes 262176 | tf_op jit(solution)/shard_map/ppermute | solution.py:139
  450.7 7.0 %collective-permute-done.8 = bf16[128,1024]{1,0:T(8,128)(2,1)S(1)} collective-permute-done((bf16[128,1024]{1,0:T(8,128)(2,1)S(1)}, bf16[128,1024]{1,0:T(8,128)(2,1)S(1)}, u32[]{:S(2)}, u32[]{:S(2)}) %collective-permute-start.8) | collective-permute-done | bytes 262176 | tf_op jit(solution)/shard_map/ppermute | solution.py:139
  457.7 7.0 %collective-permute-done.9 = bf16[128,1024]{1,0:T(8,128)(2,1)S(1)} collective-permute-done((bf16[128,1024]{1,0:T(8,128)(2,1)S(1)}, bf16[128,1024]{1,0:T(8,128)(2,1)S(1)}, u32[]{:S(2)}, u32[]{:S(2)}) %collective-permute-start.9) | collective-permute-done | bytes 262176 | tf_op jit(solution)/shard_map/ppermute | solution.py:139
  476.8 5.9 %fusion.34 = bf16[128,512]{1,0:T(8,128)(2,1)} fusion(bf16[8192,512]{1,0:T(8,128)(2,1)} %all-gather.6.cloned.1.call-done, bf16[128,16384]{1,0:T(8,128)(2,1)} %constant_dynamic-update-slice_fusion, s32[]{:T(128)S(6)} %select_n.73), kind=kOutput, calls=%fused_computation.37 | convolution fusion | flops 1073807360 | bytes 10616836 | tf_op jit(solution)/shard_map/dot_general | solution.py:143
  (246 shorter events, 132.7 us)
Async XLA Ops:
  6.5 161.4 %all-gather.8.cloned.1.call-start = ((), (), s32[]{:S(2)}) async-start(), calls=%async_computation.1 | async-start | bytes 4259840 | tf_op jit(solution)/shard_map/all_gather | solution.py:18
  7.3 13.7 %collective-permute-start.1 = (bf16[2,1024]{1,0:T(2,128)(2,1)S(1)}, bf16[2,1024]{1,0:T(2,128)(2,1)S(1)}, u32[]{:S(2)}, u32[]{:S(2)}) collective-permute-start(bf16[2,1024]{1,0:T(2,128)(2,1)S(1)} %slice.146), channel_id=1, source_target_pairs={{0,8},{8,16},{16,24},{24,32},{32,40},{40,48},{48,56},{56,64},{64,7... | collective-permute-start | bytes 12296 | tf_op jit(solution)/shard_map/ppermute | solution.py:13
  11.8 10.2 %collective-permute-start.2 = (bf16[2,1024]{1,0:T(2,128)(2,1)S(1)}, bf16[2,1024]{1,0:T(2,128)(2,1)S(1)}, u32[]{:S(2)}, u32[]{:S(2)}) collective-permute-start(bf16[2,1024]{1,0:T(2,128)(2,1)S(1)} %slice.153), channel_id=1, source_target_pairs={{0,8},{8,16},{16,24},{24,32},{32,40},{40,48},{48,56},{56,64},{64,7... | collective-permute-start | bytes 12296 | tf_op jit(solution)/shard_map/ppermute | solution.py:13
  19.2 293.0 %all-gather.10.cloned.1.call-start = ((), (), s32[]{:S(2)}) async-start(), calls=%async_computation.2 | async-start | bytes 4259840 | tf_op jit(solution)/shard_map/all_gather | solution.py:18
  32.1 36.4 %copy-start.3 = (bf16[128,1024]{1,0:T(8,128)(2,1)S(1)}, bf16[128,1024]{1,0:T(8,128)(2,1)}, u32[]{:S(2)}) copy-start(bf16[128,1024]{1,0:T(8,128)(2,1)} %param.12) | copy-start | bytes 786436
  37.3 40.0 %copy-start.2 = (f32[1024,16]{0,1:T(8,128)S(1)}, f32[1024,16]{0,1:T(8,128)}, u32[]{:S(2)}) copy-start(f32[1024,16]{0,1:T(8,128)} %param.17) | copy-start | bytes 196612
  67.8 0.6 copy-start
  67.8 9.5 %copy-start.1 = (f32[16,1024,16]{1,2,0:T(8,128)S(1)}, f32[16,1024,16]{1,2,0:T(8,128)}, u32[]{:S(2)}) copy-start(f32[16,1024,16]{1,2,0:T(8,128)} %get-tuple-element.132) | copy-start | bytes 3145732
  68.5 408.3 %all-gather.6.cloned.1.call-start = ((), (), s32[]{:S(2)}) async-start(), calls=%async_computation | async-start | bytes 8519680 | tf_op jit(solution)/shard_map/all_gather | solution.py:145
  68.5 23.3 %collective-permute-start = (bf16[2,1024]{1,0:T(2,128)(2,1)S(1)}, bf16[2,1024]{1,0:T(2,128)(2,1)S(1)}, u32[]{:S(2)}, u32[]{:S(2)}) collective-permute-start(bf16[2,1024]{1,0:T(2,128)(2,1)S(1)} %slice.138), channel_id=1, source_target_pairs={{0,8},{8,16},{16,24},{24,32},{32,40},{40,48},{48,56},{56,64},{64,7... | collective-permute-start | bytes 12296 | tf_op jit(solution)/shard_map/ppermute | solution.py:13
  415.7 7.0 %collective-permute-start.3 = (bf16[128,1024]{1,0:T(8,128)(2,1)S(1)}, bf16[128,1024]{1,0:T(8,128)(2,1)S(1)}, u32[]{:S(2)}, u32[]{:S(2)}) collective-permute-start(bf16[128,1024]{1,0:T(8,128)(2,1)S(1)} %fusion.52), channel_id=1, source_target_pairs={{0,1},{1,2},{2,3},{3,4},{4,5},{5,6},{6,7},{7,0},{8,9},{9,10},{10,1... | collective-permute-start | bytes 786440 | tf_op jit(solution)/shard_map/ppermute | solution.py:139
  422.7 7.0 %collective-permute-start.4 = (bf16[128,1024]{1,0:T(8,128)(2,1)S(1)}, bf16[128,1024]{1,0:T(8,128)(2,1)S(1)}, u32[]{:S(2)}, u32[]{:S(2)}) collective-permute-start(bf16[128,1024]{1,0:T(8,128)(2,1)S(1)} %collective-permute-done.3), channel_id=1, source_target_pairs={{0,1},{1,2},{2,3},{3,4},{4,5},{5,6},{6,7},{7,0},{8,9},{9,10},{10,1... | collective-permute-start | bytes 786440 | tf_op jit(solution)/shard_map/ppermute | solution.py:139
  429.7 7.0 %collective-permute-start.5 = (bf16[128,1024]{1,0:T(8,128)(2,1)S(1)}, bf16[128,1024]{1,0:T(8,128)(2,1)S(1)}, u32[]{:S(2)}, u32[]{:S(2)}) collective-permute-start(bf16[128,1024]{1,0:T(8,128)(2,1)S(1)} %collective-permute-done.4), channel_id=1, source_target_pairs={{0,1},{1,2},{2,3},{3,4},{4,5},{5,6},{6,7},{7,0},{8,9},{9,10},{10,1... | collective-permute-start | bytes 786440 | tf_op jit(solution)/shard_map/ppermute | solution.py:139
  436.7 7.0 %collective-permute-start.6 = (bf16[128,1024]{1,0:T(8,128)(2,1)S(1)}, bf16[128,1024]{1,0:T(8,128)(2,1)S(1)}, u32[]{:S(2)}, u32[]{:S(2)}) collective-permute-start(bf16[128,1024]{1,0:T(8,128)(2,1)S(1)} %collective-permute-done.5), channel_id=1, source_target_pairs={{0,1},{1,2},{2,3},{3,4},{4,5},{5,6},{6,7},{7,0},{8,9},{9,10},{10,1... | collective-permute-start | bytes 786440 | tf_op jit(solution)/shard_map/ppermute | solution.py:139
  443.7 7.0 %collective-permute-start.7 = (bf16[128,1024]{1,0:T(8,128)(2,1)S(1)}, bf16[128,1024]{1,0:T(8,128)(2,1)S(1)}, u32[]{:S(2)}, u32[]{:S(2)}) collective-permute-start(bf16[128,1024]{1,0:T(8,128)(2,1)S(1)} %collective-permute-done.6), channel_id=1, source_target_pairs={{0,1},{1,2},{2,3},{3,4},{4,5},{5,6},{6,7},{7,0},{8,9},{9,10},{10,1... | collective-permute-start | bytes 786440 | tf_op jit(solution)/shard_map/ppermute | solution.py:139
  450.7 7.0 %collective-permute-start.8 = (bf16[128,1024]{1,0:T(8,128)(2,1)S(1)}, bf16[128,1024]{1,0:T(8,128)(2,1)S(1)}, u32[]{:S(2)}, u32[]{:S(2)}) collective-permute-start(bf16[128,1024]{1,0:T(8,128)(2,1)S(1)} %collective-permute-done.7), channel_id=1, source_target_pairs={{0,1},{1,2},{2,3},{3,4},{4,5},{5,6},{6,7},{7,0},{8,9},{9,10},{10,1... | collective-permute-start | bytes 786440 | tf_op jit(solution)/shard_map/ppermute | solution.py:139
  457.7 7.0 %collective-permute-start.9 = (bf16[128,1024]{1,0:T(8,128)(2,1)S(1)}, bf16[128,1024]{1,0:T(8,128)(2,1)S(1)}, u32[]{:S(2)}, u32[]{:S(2)}) collective-permute-start(bf16[128,1024]{1,0:T(8,128)(2,1)S(1)} %collective-permute-done.8), channel_id=1, source_target_pairs={{0,1},{1,2},{2,3},{3,4},{4,5},{5,6},{6,7},{7,0},{8,9},{9,10},{10,1... | collective-permute-start | bytes 786440 | tf_op jit(solution)/shard_map/ppermute | solution.py:139
Sparse Core Ops, SparseCore 0:
  19.3 148.5 all-gather.7
  170.9 141.2 all-gather.9
  315.1 152.1 all-gather.5
